TPU v7x, 256 devices: a whole 4x4x8 slice. The times are simulated.
256 devices in a mesh: layer: 8 (over z_hi, x), seq: 32 (over z_lo, y, core).
Axes of the slice: x: 4, y: 4, z: 8 (z_hi: 2, z_lo: 4; z = z_hi * 4 + z_lo), core: 2. Of those that a mesh axis runs over, the one named last changes fastest.
Arguments:
- train_acts: bfloat16 [2, 256, 14336], P(None, 'seq', 'layer'), may hold values from -6 to 6
- query_acts: bfloat16 [2, 256, 14336], P(None, 'seq', 'layer'), may hold values from -6 to 6
- train_grads: bfloat16 [2, 256, 4096], P(None, 'layer', 'seq'), may hold values from -6 to 6
- query_grads: bfloat16 [2, 256, 4096], P(None, 'layer', 'seq'), may hold values from -6 to 6
- basis_in: bfloat16 [2, 14336, 14336], P(None, 'layer', 'seq'), may hold values from -0.046875 to 0.046875
- basis_out: bfloat16 [2, 4096, 4096], P(None, 'seq', 'layer'), may hold values from -0.09375 to 0.09375
- eigen: float32 [2, 4096, 14336], P(None, 'layer', 'seq'), may hold values from 0.05 to 5
- query_segment: int32 [256], replicated, may hold values from 0 to 15, never falling along the last dimension, each value on 1 to 128 neighbouring positions
Outputs:
- token_scores: float32 [16, 256], P(None, 'seq')
Inputs may be any that keep to these rules, and one draw needn't show every extreme that they name: query_segment never falls; each query has 1 to 128 tokens, one exactly 128.
All inputs are finite; a program needn't handle non-finite values.
Results may differ from a plain program's by a relative error of at most 0.0049.
Values may be sent and summed in bfloat16 or wider, within the bound.
A program may use at most 64 MiB of HBM per device.

v0:
```python
import math

import jax
import jax.numpy as jnp
from jax import lax
from jax.sharding import PartitionSpec as P

D = 4096
FF = 14336
QUERIES = 16
LAYERS = 2
QMOST = 128


DAMPING = 0.1


def split_rows(rows, groups, first):
    shaped = rows.reshape(groups, rows.shape[0] // groups, rows.shape[1])
    head_rows = shaped[:, :first].reshape(-1, rows.shape[1])
    tail_rows = shaped[:, first:].reshape(-1, rows.shape[1])
    return (head_rows, tail_rows)


def on_device(
    train_acts, query_acts, train_grads, query_grads, basis_in, basis_out, eigen, query_segment
):
    seq_count = lax.axis_size("seq")
    layer_count = lax.axis_size("layer")
    acts_train_local = train_acts.shape[1]
    grads_train_local = train_grads.shape[1]
    factor = 1.0 / math.sqrt(D * FF * QMOST)
    member = (query_segment[:, None] == jnp.arange(QUERIES, dtype=jnp.int32)[None, :]).astype(
        jnp.bfloat16
    )
    summed = jnp.zeros((QUERIES, acts_train_local), jnp.float32)
    for level in range(LAYERS):
        in_panel = basis_in[level]
        out_panel = basis_out[level]
        acts_local = jnp.concatenate([train_acts[level], query_acts[level]], axis=0)
        partial_in = jnp.dot(
            lax.all_gather(acts_local, "seq", axis=0, tiled=True),
            in_panel,
            preferred_element_type=jnp.float32,
        )
        rotated_in = lax.psum(partial_in, "layer").astype(jnp.bfloat16)
        train_in, query_in = split_rows(rotated_in, seq_count, acts_train_local)
        grads_local = jnp.concatenate([train_grads[level], query_grads[level]], axis=0)
        grads_all = lax.all_gather(grads_local, "layer", axis=0, tiled=True)
        share_out = lax.psum_scatter(
            jnp.dot(grads_all, out_panel, preferred_element_type=jnp.float32),
            "seq",
            scatter_dimension=0,
            tiled=True,
        )
        rotated_out = lax.all_gather(share_out.astype(jnp.bfloat16), "seq", axis=0, tiled=True)
        train_out, query_out = split_rows(rotated_out, layer_count, grads_train_local)
        eigen_level = eigen[level]
        train_in_wide = train_in.astype(jnp.float32)

        def one_query(column):
            masked = query_out * column[:, None]
            cross = jnp.dot(masked.T, query_in, preferred_element_type=jnp.float32)
            precond = (cross * factor / (eigen_level + DAMPING)).astype(jnp.bfloat16)
            projected = jnp.dot(train_out, precond, preferred_element_type=jnp.float32)
            return jnp.sum(projected * train_in_wide, axis=1)

        partial_scores = lax.map(one_query, member.T)
        owned = lax.psum_scatter(partial_scores, "seq", scatter_dimension=1, tiled=True)
        summed = summed + lax.psum(owned, "layer")
    return summed


def solution(mesh):
    placed = (
        P(None, "seq", "layer"),
        P(None, "seq", "layer"),
        P(None, "layer", "seq"),
        P(None, "layer", "seq"),
        P(None, "layer", "seq"),
        P(None, "seq", "layer"),
        P(None, "layer", "seq"),
        P(),
    )
    return jax.shard_map(
        on_device, mesh=mesh, in_specs=placed, out_specs=P(None, "seq"), check_vma=False
    )
```

profile of v0, /device:TPU:1, one launch (start us, length us, event | category | flops | bytes accessed | tf_op | source)
XLA Modules:
  0.0 778.3 jit_solution(16634841564788048504)
XLA Ops:
  7.3 40.4 %all_gather.21 = bf16[512,128]{1,0:T(8,128)(2,1)S(1)} all-gather(bf16[64,128]{1,0:T(8,128)(2,1)S(1)} %pad_maximum_fusion.3), channel_id=1, replica_groups=mesh['layer'=8,'seq'=32] {'layer'}, dimensions={0}, use_global_device_ids=true | all-gather | bytes 147456 | tf_op jit(solution)/shard_map/all_gather | solution.py:49
  47.8 2.2 fusion.38
  50.0 37.7 %all_gather.18 = bf16[512,128]{1,0:T(8,128)(2,1)S(1)} all-gather(bf16[64,128]{1,0:T(8,128)(2,1)S(1)} %pad_maximum_fusion.2), channel_id=1, replica_groups=mesh['layer'=8,'seq'=32] {'layer'}, dimensions={0}, use_global_device_ids=true | all-gather | bytes 147456 | tf_op jit(solution)/shard_map/all_gather | solution.py:49
  87.8 1.3 fusion.40
  92.9 104.1 %reduce-scatter.5.cloned.1.call-done = f32[16,512]{1,0:T(8,128)} async-done(((f32[512,512]{1,0:T(8,128)}), f32[16,512]{1,0:T(8,128)}) %reduce-scatter.5.cloned.1.call-update) | async-done | bytes 32784 | tf_op jit(solution)/shard_map/reduce_scatter | solution.py:50
  197.8 142.7 %reduce-scatter.3.cloned.1.call-done = f32[16,512]{1,0:T(8,128)} async-done(((f32[512,512]{1,0:T(8,128)}), f32[16,512]{1,0:T(8,128)}) %reduce-scatter.3.cloned.1.call-update) | async-done | bytes 32784 | tf_op jit(solution)/shard_map/reduce_scatter | solution.py:50
  341.3 45.0 %all_gather.22 = bf16[512,512]{1,0:T(8,128)(2,1)S(1)} all-gather(bf16[16,512]{1,0:T(8,128)(2,1)S(1)} %convert_element_type.39), channel_id=1, replica_groups=mesh['layer'=8,'seq'=32] {'seq'}, dimensions={0}, use_global_device_ids=true | all-gather | bytes 540672 | tf_op jit(solution)/shard_map/all_gather | solution.py:56
  387.2 41.5 %all_gather.19 = bf16[512,512]{1,0:T(8,128)(2,1)S(1)} all-gather(bf16[16,512]{1,0:T(8,128)(2,1)S(1)} %convert_element_type.35), channel_id=1, replica_groups=mesh['layer'=8,'seq'=32] {'seq'}, dimensions={0}, use_global_device_ids=true | all-gather | bytes 540672 | tf_op jit(solution)/shard_map/all_gather | solution.py:56
  429.5 3.0 fusion.30
  432.6 32.5 %all-gather.3.cloned.1.call-done = bf16[512,1792]{1,0:T(8,128)(2,1)} async-done(((bf16[16,1792]{1,0:T(8,128)(2,1)}), bf16[512,1792]{1,0:T(8,128)(2,1)}) %all-gather.3.cloned.1.call-update) | async-done | bytes 1835024 | tf_op jit(solution)/shard_map/all_gather | solution.py:42
  465.0 3.0 fusion.32
  468.0 103.1 %all-reduce.3 = (bf16[512,448]{0,1:T(8,128)(2,1)S(1)}, bf16[512,448]{0,1:T(8,128)(2,1)}) all-reduce(f32[512,448]{0,1:T(8,128)S(1)} %fusion.32, f32[512,448]{0,1:T(8,128)S(1)} %fusion.30), channel_id=1, replica_groups=mesh['layer'=8,'seq'=32] {'layer'}, use_global_device_ids=true, to_apply=%region_1.0 | all-reduce | flops 458752 | bytes 2752512 | tf_op jit(solution)/shard_map/psum | solution.py:46
  573.5 27.5 %while.21 = (s32[]{:T(128)}, f32[16,256]{1,0:T(8,128)S(1)}, bf16[16,256]{1,0:T(8,128)(2,1)S(1)}, bf16[256,512]{1,0:T(8,128)(2,1)}, bf16[256,448]{1,0:T(8,128)(2,...) while((s32[]{:T(128)}, f32[16,256]{1,0:T(8,128)S(1)}, ...), condition=%wide.region_11.12_spmd, body=%wide.region_9.11_spmd.sunk | while | flops 236158720 | bytes 2134637 | solution.py:68
  573.5 1.6 fusion.70
  575.2 1.6 fusion.70
  576.9 1.6 fusion.70
  578.7 1.6 fusion.70
  580.4 1.6 fusion.70
  582.1 1.6 fusion.70
  583.8 1.6 fusion.70
  585.5 1.6 fusion.70
  587.3 1.6 fusion.70
  589.0 1.6 fusion.70
  590.7 1.6 fusion.70
  592.4 1.6 fusion.70
  594.1 1.6 fusion.70
  595.9 1.6 fusion.70
  597.6 1.6 fusion.70
  599.3 1.6 fusion.70
  602.0 9.9 %while.20 = (s32[]{:T(128)}, f32[16,256]{1,0:T(8,128)S(1)}, bf16[16,256]{1,0:T(8,128)(2,1)S(1)}, bf16[256,512]{1,0:T(8,128)(2,1)S(1)}, bf16[256,448]{1,0:T(8,128...) while((s32[]{:T(128)}, f32[16,256]{1,0:T(8,128)S(1)}, ...), condition=%wide.region_4.5_spmd, body=%wide.region_2.4_spmd.sunk | while | flops 236158720 | bytes 2134637 | solution.py:68
  612.0 135.4 %all-reduce = f32[16,256]{0,1:T(8,128)S(1)} all-reduce(f32[16,256]{0,1:T(8,128)S(1)} %copy.33), channel_id=5, replica_groups=mesh['layer'=8,'seq'=32] {'seq'}, use_global_device_ids=true, to_apply=%region_5.6.clone | all-reduce | flops 4096 | bytes 32768
  747.4 24.4 %psum.32 = f32[16,8]{0,1:T(8,128)} all-reduce(f32[16,8]{0,1:T(8,128)S(1)} %constant_dynamic-slice_fusion), channel_id=1, replica_groups=mesh['layer'=8,'seq'=32] {'layer'}, use_global_device_ids=true, to_apply=%region_6.7 | all-reduce | flops 128 | bytes 1024 | tf_op jit(solution)/shard_map/psum | solution.py:70
  (131 shorter events, 21.1 us)
Async XLA Ops:
  6.5 81.2 %copy-start.2 = (bf16[2,128,512]{2,1,0:T(8,128)(2,1)S(1)}, bf16[2,128,512]{2,1,0:T(8,128)(2,1)}, u32[]{:S(2)}) copy-start(bf16[2,128,512]{2,1,0:T(8,128)(2,1)} %param.17) | copy-start | bytes 786436
  6.5 190.5 %reduce-scatter.5.cloned.1.call-start = ((), (), s32[]{:S(2)}) async-start(), calls=%async_computation.4 | async-start | bytes 1081344 | tf_op jit(solution)/shard_map/reduce_scatter | solution.py:50
  49.9 39.3 %copy-start.5 = (bf16[2,8,1792]{2,1,0:T(8,128)(2,1)S(1)}, bf16[2,8,1792]{2,1,0:T(8,128)(2,1)}, u32[]{:S(2)}) copy-start(bf16[2,8,1792]{2,1,0:T(8,128)(2,1)} %param.13) | copy-start | bytes 172036
  49.9 39.3 %copy-start.6 = (bf16[2,8,1792]{2,1,0:T(8,128)(2,1)S(1)}, bf16[2,8,1792]{2,1,0:T(8,128)(2,1)}, u32[]{:S(2)}) copy-start(bf16[2,8,1792]{2,1,0:T(8,128)(2,1)} %param.12) | copy-start | bytes 172036
  49.9 40.6 %copy-start.8 = (u32[256]{0:T(256)S(1)}, u32[256]{0:T(256)}, u32[]{:S(2)}) copy-start(u32[256]{0:T(256)} %constant.36) | copy-start | bytes 3076
  49.9 41.9 %copy-start.7 = (s32[256]{0:T(256)S(1)}, s32[256]{0:T(256)}, u32[]{:S(2)}) copy-start(s32[256]{0:T(256)} %param.19) | copy-start | bytes 3076
  50.0 41.9 %copy-start = (f32[2,512,448]{1,2,0:T(8,128)S(1)}, f32[2,512,448]{1,2,0:T(8,128)}, u32[]{:S(2)}) copy-start(f32[2,512,448]{1,2,0:T(8,128)} %param.18) | copy-start | bytes 5505028
  50.0 290.6 %reduce-scatter.3.cloned.1.call-start = ((), (), s32[]{:S(2)}) async-start(), calls=%async_computation.2 | async-start | bytes 1081344 | tf_op jit(solution)/shard_map/reduce_scatter | solution.py:50
  89.1 340.4 %all-gather.5.cloned.1.call-start = ((), (), s32[]{:S(2)}) async-start(), calls=%async_computation.5 | async-start | bytes 1892352 | tf_op jit(solution)/shard_map/all_gather | solution.py:42
  89.9 375.2 %all-gather.3.cloned.1.call-start = ((), (), s32[]{:S(2)}) async-start(), calls=%async_computation.3 | async-start | bytes 1892352 | tf_op jit(solution)/shard_map/all_gather | solution.py:42
  571.2 2.3 copy-start.1
  601.0 1.0 copy-start.3
  601.0 1.0 copy-start.4
Sparse Core Ops, SparseCore 0:
  50.1 146.9 reduce-scatter.4
  199.7 140.7 reduce-scatter.2
  342.4 61.9 all-gather.4
  406.1 58.8 all-gather.2
where the time goes:
time: 789 us; the launch traced here: 778 us
  blocking collectives  428 us (54%)
  waiting for transfers between devices  279 us (35%)
  matrix products  43.9 us (6%)
  between operations  14 us (2%)
  local copies, waits for them, and re-layouts  8.9 us (1%)
    reduce_scatter x2, waiting for transfers between devices, on_device(): lax.psum_scatter(jnp.dot(grads_all, out_panel, preferred_element_type=jnp...  247 us
    unnamed x1, blocking collectives  135 us
    psum x1, blocking collectives, on_device(): rotated_in = lax.psum(partial_in, 'layer').astype(jnp.bfloat16)  103 us
    all_gather x2, blocking collectives, on_device(): lax.all_gather(share_out.astype(jnp.bfloat16), 'seq', axis=0, tiled=True)  86.5 us
    all_gather x2, blocking collectives, on_device(): grads_all = lax.all_gather(grads_local, 'layer', axis=0, tiled=True)  78.2 us
    dot_general x32, matrix products, one_query(): projected = jnp.dot(train_out, precond, preferred_element_type=jnp.float32)  34.4 us
    all_gather x2, waiting for transfers between devices, on_device(): lax.all_gather(acts_local, 'seq', axis=0, tiled=True)  32.5 us
    psum x1, blocking collectives, on_device(): summed = summed + lax.psum(owned, 'layer')  24.4 us
  transfers between devices with their start and end apart: 4, of which 3 were waited for; matrix products, arithmetic and copies ran while one was open for 1% of the time, Pallas kernels for 0%

commit v1 on v0

v1 whole, which is shorter than its diff:
```python
import functools
import math

import jax
import jax.numpy as jnp
from jax import lax
from jax.experimental import pallas as pl
from jax.experimental.pallas import tpu as pltpu
from jax.sharding import PartitionSpec as P

D = 4096
FF = 14336
QUERIES = 16
LAYERS = 2
QMOST = 128
DAMPING = 0.1

MESH = pl.DeviceIdType.MESH
BF16 = jnp.bfloat16
F32 = jnp.float32

HI, X, Z, Y, CORE = 2, 4, 4, 4, 2
TOK = 256
ROWS_IN = FF // (HI * X)
COLS_IN = FF // (Z * Y * CORE)
ROWS_OUT = D // (Z * Y * CORE)
COLS_OUT = D // (HI * X)
COPIES = 128
PIECE = COLS_IN // X
GROUP = 16
VMEM_LIMIT = 62 * 1024 * 1024
NT = (((1,), (1,)), ((), ()))


class Links:
    def __init__(self, send_sem, recv_sem, peer):
        self.send_sem, self.recv_sem, self.peer = send_sem, recv_sem, peer
        self.sent = []
        self.pooled = 0
        self.finished = 0

    def start(self, src, dst, peer, recv=None, again=None):
        if recv is None:
            recv = self.recv_sem.at[self.pooled]
            self.pooled += 1
        copy = pltpu.make_async_remote_copy(
            src_ref=src,
            dst_ref=dst,
            send_sem=self.send_sem.at[len(self.sent)],
            recv_sem=recv,
            device_id=peer,
            device_id_type=MESH,
        )
        copy.start()
        self.sent.append(again or (lambda: src))
        return copy

    def landed(self, block, recv, peer):
        pltpu.make_async_remote_copy(
            src_ref=block,
            dst_ref=block,
            send_sem=self.send_sem.at[0],
            recv_sem=recv,
            device_id=peer,
            device_id_type=MESH,
        ).wait_recv()

    def finish(self):
        for at in range(self.finished, len(self.sent)):
            block = self.sent[at]()
            pltpu.make_async_remote_copy(
                src_ref=block,
                dst_ref=block,
                send_sem=self.send_sem.at[at],
                recv_sem=self.recv_sem.at[0],
                device_id=self.peer,
                device_id_type=MESH,
            ).wait_send()
        self.finished = len(self.sent)


def received(copies):
    for copy in copies:
        copy.wait_recv()


def kernel(
    ta_hbm, qa_hbm, tg_hbm, qg_hbm, bo_hbm, seg_hbm, bi_hbm, eig_hbm,
    out_ref,
    ta, qa, seg, bi, eig, tokens, acts, grads_s, grads, bo,
    part_out, own_out, ry, rz_s, rz, out_t,
    part_in, rx_s, rx, zs, zr, give, rin,
    scores, es1, er1, es2, er2, es3, er3,
    local_sem, send_sem, recv_sem, z_sem, y_sem, on_sem, piece_sem, x_sem, hi_sem, hand_sem, give_sem,
):
    li = lax.axis_index("layer")
    si = lax.axis_index("seq")
    hi, x = li // X, li % X
    z, y, core = si // (Y * CORE), (si // CORE) % Y, si % CORE
    other = 1 - core
    factor = 1.0 / math.sqrt(D * FF * QMOST)

    def device(hh, xx, zz, yy, cc):
        return {"layer": hh * X + xx, "seq": (zz * Y + yy) * CORE + cc}

    z_of = [lax.rem(z + d, Z) for d in range(Z)]
    y_of = [lax.rem(y + d, Y) for d in range(Y)]
    x_of = [lax.rem(x + d, X) for d in range(X)]
    ring_of = [lax.rem(hi * Z + z + d, HI * Z) for d in range(HI * Z)]
    mate = device(hi, x, z, y, other)
    z_peer = [device(hi, x, z_of[d], y, core) for d in range(Z)]
    y_peer = [device(hi, x, z, y_of[d], core) for d in range(Y)]
    x_peer = [device(hi, x_of[d], z, y, core) for d in range(X)]
    x_other = [device(hi, x_of[d], z, y, other) for d in range(X)]
    hi_peer = device(1 - hi, x, z, y, core)
    hi_other = device(1 - hi, x, z, y, other)
    ring_peer = [device(at // Z, x, at % Z, y, core) for at in ring_of]
    links = Links(send_sem, recv_sem, mate)

    barrier = pltpu.get_barrier_semaphore()
    peers = [mate, hi_other] + ring_peer[1:] + y_peer[1:] + x_peer[1:] + x_other[1:]
    for peer in peers:
        pl.semaphore_signal(barrier, inc=1, device_id=peer, device_id_type=MESH)

    bo_span = pl.ds(pl.multiple_of(core * ROWS_OUT, ROWS_OUT), ROWS_OUT)
    moves = [(ta_hbm, ta), (qa_hbm, qa), (tg_hbm, grads_s.at[0]), (qg_hbm, grads_s.at[1])]
    moves += [(bo_hbm, bo.at[:, bo_span, :]), (seg_hbm, seg)]
    moves += [(bi_hbm.at[level], bi.at[level, core]) for level in range(LAYERS)]
    moves += [(eig_hbm.at[level], eig.at[level]) for level in range(LAYERS)]
    loads = []
    for at, (src, dst) in enumerate(moves):
        loads.append(pltpu.make_async_copy(src, dst, local_sem.at[at]))
        loads[-1].start()

    for load in loads[:2]:
        load.wait()
    rows = ta.shape[0] // LAYERS
    for level in range(LAYERS):
        span = slice(level * rows, (level + 1) * rows)
        block = jnp.concatenate([ta[...].astype(F32)[span], qa[...].astype(F32)[span]], axis=0)
        acts[level, z, y] = block.astype(BF16)

    def sort_segments():
        wide = jnp.broadcast_to(seg[...].astype(F32), (8, TOK)).astype(BF16)
        old = lax.broadcasted_iota(jnp.int32, (TOK, TOK), 0)
        new = lax.broadcasted_iota(jnp.int32, (TOK, TOK), 1)
        half = TOK // CORE
        source = (new % half) // rows * (rows * CORE) + new // half * rows + new % rows
        pick = (old == source).astype(F32).astype(BF16)
        return jnp.dot(wide, pick, preferred_element_type=F32)[:1]

    pl.semaphore_wait(barrier, len(peers))

    nearest = z - 1 + 2 * (1 - (z + Z - 1) // Z)
    farthest = 3 * (1 - z // 2)
    order = [z, nearest, 6 - z - nearest - farthest, farthest]

    def along_z(level):
        block = acts.at[level, z, y]
        for at in order[1:]:
            links.start(block, block, device(hi, x, at, y, core), z_sem.at[level, z])

    def along_y(level, k):
        block = acts.at[level, order[k], y]
        links.start(block, block, y_peer[1], y_sem.at[level, 0, order[k]])
        links.start(block, block, y_peer[3], y_sem.at[level, 1, order[k]])

    def spread(level, k):
        links.landed(acts.at[level, order[k], y], z_sem.at[level, order[k]], mate)
        along_y(level, k)

    def pass_on(level, k):
        left = acts.at[level, order[k], y_of[3]]
        right = acts.at[level, order[k], y_of[1]]
        links.landed(left, y_sem.at[level, 0, order[k]], mate)
        if k % 2 == 0:
            links.start(left, left, y_peer[1], on_sem.at[level, order[k]])
        links.landed(right, y_sem.at[level, 1, order[k]], mate)
        if k % 2 == 1:
            links.start(right, right, y_peer[3], on_sem.at[level, order[k]])

    def gathered(level):
        for k in range(Z):
            links.landed(acts.at[level, order[k], y_of[2]], on_sem.at[level, order[k]], mate)

    y_rows = TOK // Y
    z_rows = y_rows // Z

    def rotate_out(level):
        own = grads[level].reshape(TOK, CORE * ROWS_OUT)
        product = jnp.dot(own, bo[level], preferred_element_type=F32)
        product = product.reshape(TOK // (CORE * rows), CORE, rows, COLS_OUT)
        product = jnp.swapaxes(product, 0, 1).reshape(TOK, COLS_OUT)
        part_out[level] = product
        own_out[level] = product.astype(BF16).reshape(Y, y_rows, COLS_OUT)
        return [
            links.start(own_out.at[level, y_of[d]], ry.at[level, d - 1], y_peer[d])
            for d in (2, 1, 3)
        ]

    def add_y(level, starts):
        received(starts)
        total = part_out[level, pl.ds(pl.multiple_of(y * y_rows, y_rows), y_rows), :]
        for d in range(Y - 1):
            total = total + ry[level, d].astype(F32)
        rz_s[level] = total.reshape(Z, z_rows, COLS_OUT)
        return [
            links.start(rz_s.at[level, z_of[d]], rz.at[level, d - 1], z_peer[d])
            for d in (2, 1, 3)
        ]

    def add_z(level, starts):
        received(starts)
        total = rz_s[level, z]
        for d in range(Z - 1):
            total = total + rz[level, d]
        out_t[core, level, y, z] = total.astype(BF16)
        block = out_t.at[core, level, y, z]
        return [links.start(block, block, z_peer[d]) for d in (2, 1, 3)]

    def gather_y(level, starts):
        received(starts)
        block = out_t.at[core, level, y]
        return [links.start(block, block, y_peer[d]) for d in (2, 1, 3)]

    def hand_over(level, starts):
        received(starts)
        block = out_t.at[core, level]
        links.start(block, block, mate, hand_sem.at[level], lambda: out_t.at[core, level])

    def handed(level):
        links.landed(out_t.at[other, level], hand_sem.at[level], mate)

    def prepare(level):
        loads[8 + level].wait()
        eig[level] = factor / (eig[level] + DAMPING)

    def rotate(level):
        @pl.loop(0, TOK // 32)
        def _(p):
            pair = acts[level, p // (Y // 2), pl.ds(p % (Y // 2) * 2, 2)].astype(F32)
            for at in range(2):
                piece = pair[:, at * rows:(at + 1) * rows].reshape(2 * rows, ROWS_IN)
                here = pl.ds(pl.multiple_of(at * (TOK // 2) + p * 2 * rows, 2 * rows), 2 * rows)
                tokens[here, :] = piece.astype(BF16)

        @pl.loop(0, CORE)
        def _(c):
            product = lax.dot_general(bi[level, c], tokens[...], NT, preferred_element_type=F32)
            part_in[level, c] = product.reshape(X, PIECE, TOK)
            rx_s[level, c] = product.astype(BF16).reshape(X, PIECE, TOK)
            for k in range(CORE):
                @pl.when(c == k)
                def _(k=k):
                    for d in (2, 1, 3):
                        links.start(
                            rx_s.at[level, k, x_of[d]], rx.at[level, k, d - 1], x_peer[d],
                            x_sem.at[level, k, d - 1], lambda: zs.at[level, k],
                        )

    def add_x(level, c):
        for d in range(X - 1):
            links.landed(rx.at[level, c, d], x_sem.at[level, c, d], mate)
        total = part_in[level, c, x]
        for d in range(X - 1):
            total = total + rx[level, c, d].astype(F32)
        part_in[level, c, x] = total
        zs[level, c] = total.astype(BF16)
        links.start(
            zs.at[level, c], zr.at[level, c], hi_peer, hi_sem.at[level, c],
            lambda: zs.at[level, c],
        )

    def add_hi(level, c):
        links.landed(zr.at[level, c], hi_sem.at[level, c], mate)
        total = part_in[level, c, x] + zr[level, c].astype(F32)
        give[level, c] = total.astype(BF16)

        @pl.when(core == c)
        def _():
            rin[level, core, x] = give[level, c]

        @pl.when(core != c)
        def _():
            pltpu.make_async_remote_copy(
                src_ref=give.at[level, c],
                dst_ref=rin.at[level, core, x],
                send_sem=give_sem.at[level],
                recv_sem=piece_sem.at[level, 0, core],
                device_id=mate,
                device_id_type=MESH,
            ).start()

        for d in (1, 2, 3):
            links.start(
                give.at[level, c], rin.at[level, core, x], device(hi, x_of[d], z, y, c),
                piece_sem.at[level, d, core], lambda: give.at[level, c],
            )

    along_y(0, 0)
    along_z(0)
    for load in loads[2:6]:
        load.wait()
    theirs = grads.at[:, hi, x, :, bo_span]
    grads_in = [
        links.start(grads_s.at[core], theirs, hi_peer),
        links.start(grads_s.at[other], theirs, hi_other),
        links.start(grads_s.at[other], theirs, mate),
    ]
    along_y(1, 0)
    bo_swap = links.start(bo.at[:, bo_span, :], bo.at[:, bo_span, :], mate)
    bi_swap = [links.start(bi_hbm.at[level], bi.at[level, core], mate) for level in range(LAYERS)]
    for c in range(CORE):
        @pl.when(core == c)
        def _(c=c):
            grads[:, hi, x, :, pl.ds(c * ROWS_OUT, ROWS_OUT)] = grads_s[c]

    segment = sort_segments()

    spread(0, 1)
    along_z(1)
    pass_on(0, 0)
    received(grads_in)
    block = grads.at[:, :, x]
    grads_x = [links.start(block, block, x_peer[d]) for d in (2, 1, 3)]
    spread(0, 2)
    pass_on(0, 1)
    prepare(0)
    received([bo_swap])
    spread(0, 3)
    received(grads_x)
    out = [rotate_out(0), None]
    pass_on(0, 2)
    pass_on(0, 3)
    pass_on(1, 0)
    spread(1, 1)
    spread(1, 2)
    spread(1, 3)
    out[1] = rotate_out(1)
    out[0] = add_y(0, out[0])
    gathered(0)
    loads[6].wait()
    received(bi_swap[:1])
    rotate(0)

    pass_on(1, 1)
    pass_on(1, 2)
    out[0] = add_z(0, out[0])
    pass_on(1, 3)
    out[1] = add_y(1, out[1])
    out[0] = gather_y(0, out[0])
    add_x(0, 0)
    add_x(0, 1)
    out[1] = add_z(1, out[1])
    prepare(1)
    gathered(1)
    loads[7].wait()
    received(bi_swap[1:])
    rotate(1)
    hand_over(0, out[0])
    out[1] = gather_y(1, out[1])
    add_hi(0, 0)
    add_hi(0, 1)
    add_x(1, 0)
    handed(0)


    scores[...] = jnp.zeros_like(scores)

    @pl.loop(0, LAYERS * X)
    def _(step):
        level, d = step // X, step % X
        at = lax.rem(x + X - d, X)

        @pl.when(step == 1)
        def _():
            add_x(1, 1)
            hand_over(1, out[1])

        @pl.when(step == 3)
        def _():
            add_hi(1, 0)

        @pl.when(step == 4)
        def _():
            add_hi(1, 1)
            handed(1)

        links.landed(rin.at[level, other, at], piece_sem.at[level, d, other], mate)

        @pl.when(d != 0)
        def _():
            links.landed(rin.at[level, core, at], piece_sem.at[level, d, core], mate)

        both = [rin[level, c, at] for c in range(CORE)]
        train_in = jnp.concatenate([b[:, :TOK // 2] for b in both], axis=1).astype(F32)
        query_in = jnp.concatenate([b[:, TOK // 2:] for b in both], axis=1)
        scale = eig[level, pl.ds(pl.multiple_of(at * PIECE, PIECE), PIECE), :]
        query_out = out_t[1, level].reshape(TOK, COLS_OUT)
        train_out = out_t[0, level].reshape(TOK, COLS_OUT)

        @pl.loop(0, QUERIES // GROUP)
        def _(g):
            masked = []
            for k in range(GROUP):
                member = (segment == (g * GROUP + k).astype(F32)).astype(F32).astype(BF16)
                masked.append(query_in * member)
            masked = jnp.concatenate(masked, axis=0)
            cross = jnp.dot(masked, query_out, preferred_element_type=F32)
            cross = cross.reshape(GROUP, PIECE, COLS_OUT) * scale[None]
            precond = cross.astype(BF16).reshape(GROUP * PIECE, COLS_OUT)
            right = lax.dot_general(precond, train_out, NT, preferred_element_type=F32)
            right = right.reshape(GROUP, PIECE, TOK) * train_in[None]
            right = jnp.sum(right.reshape(GROUP, PIECE // 8, 8, TOK), axis=1)
            here = pl.ds(g * GROUP, GROUP)
            scores[here] = scores[here] + right

    summed = jnp.sum(scores[...], axis=1)
    half = TOK // 2
    es1[0] = summed[:, :half]
    es1[1] = summed[:, half:]
    ends = []
    for d in (2, 1, 3):
        ends.append(links.start(es1.at[other], er1.at[X - 1 + d], x_other[d]))
        ends.append(links.start(es1.at[core], er1.at[d], x_peer[d]))
    ends.append(links.start(es1.at[other], er1.at[0], mate))
    links.finish()
    for level in range(LAYERS):
        pltpu.make_async_remote_copy(
            src_ref=give.at[level, 0],
            dst_ref=give.at[level, 0],
            send_sem=give_sem.at[level],
            recv_sem=recv_sem.at[0],
            device_id=mate,
            device_id_type=MESH,
        ).wait_send()
    received(ends)
    total = es1[core]
    for d in range(X * CORE - 1):
        total = total + er1[d]
    es2[...] = total
    ends = []
    for d in (4, 3, 5, 2, 6, 1, 7):
        ends.append(links.start(es2, er2.at[d - 1], ring_peer[d]))
    received(ends)
    for d in range(HI * Z - 1):
        total = total + er2[d]
    es3[...] = total
    ends = [links.start(es3, er3.at[d - 1], y_peer[d]) for d in (2, 1, 3)]
    received(ends)
    for d in range(Y - 1):
        total = total + er3[d]
    out_ref[...] = total
    links.finish()


def fused(ta, qa, tg, qg, basis_in, basis_out, eigen, segment):
    y_rows = TOK // Y
    z_rows = y_rows // Z
    half = TOK // 2
    scratch = [
        pltpu.VMEM((16, ROWS_IN), BF16),
        pltpu.VMEM((16, ROWS_IN), BF16),
        pltpu.VMEM((1, TOK), jnp.int32),
        pltpu.VMEM((LAYERS, CORE, COLS_IN, ROWS_IN), BF16),
        pltpu.VMEM((LAYERS, COLS_IN, COLS_OUT), F32),
        pltpu.VMEM((TOK, ROWS_IN), BF16),
        pltpu.VMEM((LAYERS, Z, Y, 16, ROWS_IN), BF16),
        pltpu.VMEM((2, LAYERS, 32, ROWS_OUT), BF16),
        pltpu.VMEM((LAYERS, HI, X, 32, CORE * ROWS_OUT), BF16),
        pltpu.VMEM((LAYERS, CORE * ROWS_OUT, COLS_OUT), BF16),
        pltpu.VMEM((LAYERS, TOK, COLS_OUT), F32),
        pltpu.VMEM((LAYERS, Y, y_rows, COLS_OUT), BF16),
        pltpu.VMEM((LAYERS, Y - 1, y_rows, COLS_OUT), BF16),
        pltpu.VMEM((LAYERS, Z, z_rows, COLS_OUT), F32),
        pltpu.VMEM((LAYERS, Z - 1, z_rows, COLS_OUT), F32),
        pltpu.VMEM((2, LAYERS, Y, Z, z_rows, COLS_OUT), BF16),
        pltpu.VMEM((LAYERS, 2, X, PIECE, TOK), F32),
        pltpu.VMEM((LAYERS, 2, X, PIECE, TOK), BF16),
        pltpu.VMEM((LAYERS, 2, X - 1, PIECE, TOK), BF16),
        pltpu.VMEM((LAYERS, 2, PIECE, TOK), BF16),
        pltpu.VMEM((LAYERS, 2, PIECE, TOK), BF16),
        pltpu.VMEM((LAYERS, CORE, PIECE, TOK), BF16),
        pltpu.VMEM((LAYERS, 2, X, PIECE, TOK), BF16),
        pltpu.VMEM((QUERIES, 8, TOK), F32),
        pltpu.VMEM((2, QUERIES, half), F32),
        pltpu.VMEM((HI * Z - 1, QUERIES, half), F32),
        pltpu.VMEM((QUERIES, half), F32),
        pltpu.VMEM((Y * CORE - 1, QUERIES, half), F32),
        pltpu.VMEM((QUERIES, half), F32),
        pltpu.VMEM((X - 1, QUERIES, half), F32),
        pltpu.SemaphoreType.DMA((6 + 2 * LAYERS,)),
        pltpu.SemaphoreType.DMA((COPIES,)),
        pltpu.SemaphoreType.DMA((COPIES,)),
        pltpu.SemaphoreType.DMA((LAYERS, Z)),
        pltpu.SemaphoreType.DMA((LAYERS, 2, Z)),
        pltpu.SemaphoreType.DMA((LAYERS, Z)),
        pltpu.SemaphoreType.DMA((LAYERS, X, 2)),
        pltpu.SemaphoreType.DMA((LAYERS, CORE, X - 1)),
        pltpu.SemaphoreType.DMA((LAYERS, CORE)),
        pltpu.SemaphoreType.DMA((LAYERS,)),
        pltpu.SemaphoreType.DMA((LAYERS,)),
    ]
    return pl.pallas_call(
        kernel,
        out_shape=jax.ShapeDtypeStruct((QUERIES, half), F32),
        in_specs=[pl.BlockSpec(memory_space=pl.ANY)] * 8,
        out_specs=pl.BlockSpec(memory_space=pltpu.VMEM),
        scratch_shapes=scratch,
        compiler_params=pltpu.CompilerParams(
            collective_id=0, has_side_effects=True, vmem_limit_bytes=VMEM_LIMIT
        ),
        cost_estimate=pl.CostEstimate(flops=9_400_000_000, bytes_accessed=6_000_000, transcendentals=0),
    )(ta, qa, tg, qg, basis_out, segment, basis_in, eigen)


def on_device(
    train_acts, query_acts, train_grads, query_grads, basis_in, basis_out, eigen, query_segment
):
    half = fused(
        train_acts.reshape(-1, ROWS_IN),
        query_acts.reshape(-1, ROWS_IN),
        train_grads,
        query_grads,
        jnp.swapaxes(basis_in, 1, 2),
        basis_out,
        jnp.swapaxes(eigen, 1, 2),
        query_segment.reshape(1, TOK),
    )
    own = TOK // (Z * Y * CORE)
    start = lax.axis_index("seq") // CORE * own
    return lax.dynamic_slice(half, (0, start), (QUERIES, own))


def solution(mesh):
    placed = (
        P(None, "seq", "layer"),
        P(None, "seq", "layer"),
        P(None, "layer", "seq"),
        P(None, "layer", "seq"),
        P(None, "layer", "seq"),
        P(None, "seq", "layer"),
        P(None, "layer", "seq"),
        P(),
    )
    return jax.shard_map(
        on_device, mesh=mesh, in_specs=placed, out_specs=P(None, "seq"), check_vma=False
    )
```

time: 789 us -> 82.4 us (0.10); the launches traced: 778 us -> 82.1 us
  blocking collectives: 428 us -> 0 us
  waiting for transfers between devices: 279 us -> 0 us
  Pallas kernels: 0 us -> 80.7 us
  matrix products: 43.9 us -> 0 us
  between operations: 14 us -> 0.01 us
    reduce_scatter x2 -> x0, waiting for transfers between devices: 247 us -> none  [on_device(): lax.psum_scatter(jnp.dot(grads_all, out_panel, preferred_element_type=jnp...]
    all_gather x4 -> x0, blocking collectives: 165 us -> none  [the longest x2 86.5 us: on_device(): lax.all_gather(share_out.astype(jnp.bfloat16), 'seq', axis=0, tiled=True)]
    unnamed x1 -> x0, blocking collectives: 135 us -> none
    psum x2 -> x0, blocking collectives: 128 us -> none  [the longest x1 103 us: on_device(): rotated_in = lax.psum(partial_in, 'layer').astype(jnp.bfloat16)]
    pallas_call x0 -> x1, Pallas kernels: none -> 80.7 us  [fused(): pl.pallas_call(kernel, out_shape=jax.ShapeDtypeStruct((QUERIES, half), F3...]
    dot_general x36 -> x0, matrix products: 43.9 us -> none  [the longest x32 34.4 us: one_query(): projected = jnp.dot(train_out, precond, preferred_element_type=jnp.float32)]
    all_gather x2 -> x0, waiting for transfers between devices: 32.5 us -> none  [on_device(): lax.all_gather(acts_local, 'seq', axis=0, tiled=True)]
  transfers between devices with their start and end apart: 4 -> 0, of which waited for: 3 -> 0; matrix products, arithmetic and copies ran while one was open for 1% -> 0% of each run, Pallas kernels for 0% -> 0%
where the time goes in v1:
time: 82.4 us; the launch traced here: 82.1 us
  Pallas kernels  80.7 us (98%)
  local copies, waits for them, and re-layouts  1.44 us (2%)
    pallas_call x1, Pallas kernels, fused(): pl.pallas_call(kernel, out_shape=jax.ShapeDtypeStruct((QUERIES, half), F3...  80.7 us

profile of v1, /device:TPU:1, one launch (start us, length us, event | category | flops | bytes accessed | tf_op | source)
XLA Modules:
  0.0 82.1 jit_solution(5763394071416523302)
XLA Ops:
  0.0 80.7 %shard_map.82 = f32[16,128]{1,0:T(8,128)} custom-call(bf16[16,1792]{1,0:T(8,128)(2,1)} %bitcast.7, bf16[16,1792]{1,0:T(8,128)(2,1)} %bitcast.8, bf16[2,32,128]{2,1,0:T(8,128)(2,1)} %tg_hbm.1, bf16[2,32,128]{2,1,0:T(8,128)(2,1)} %qg_hbm.1, bf16[2,128,512]{2,1,0:T(8,128)(2,1)} %bo_hbm.1, s32[1,256]{1,0:T(1,128)} %bitcast.9, bf16[2,448,1792]{2,1,0:T(8,128)(2,1)} %bitcast.5, ...), custom_call_target="tpu_custom_call" | custom-call | flops 9400000512 | bytes 6000000 | tf_op jit(solution)/shard_map/pallas_call | solution.py:504
  80.7 0.8 constant_dynamic-slice_fusion
  81.5 0.7 copy.9

commit v2 on v1

--- a/solution.py
+++ b/solution.py
@@ -91,7 +91,7 @@
     part_out, own_out, ry, rz_s, rz, out_t,
     part_in, rx_s, rx, zs, zr, give, rin,
     scores, es1, er1, es2, er2, es3, er3,
-    local_sem, send_sem, recv_sem, z_sem, y_sem, on_sem, piece_sem, x_sem, hi_sem, hand_sem, give_sem,
+    local_sem, send_sem, recv_sem, z_sem, y_sem, on_sem, piece_sem, x_sem, hi_sem, hand_sem, give_sem, out_sem,
 ):
     li = lax.axis_index("layer")
     si = lax.axis_index("seq")
@@ -155,10 +155,9 @@
     farthest = 3 * (1 - z // 2)
     order = [z, nearest, 6 - z - nearest - farthest, farthest]
 
-    def along_z(level):
+    def along_z(level, k):
         block = acts.at[level, z, y]
-        for at in order[1:]:
-            links.start(block, block, device(hi, x, at, y, core), z_sem.at[level, z])
+        links.start(block, block, device(hi, x, order[k], y, core), z_sem.at[level, z])
 
     def along_y(level, k):
         block = acts.at[level, order[k], y]
@@ -220,11 +219,15 @@
 
     def gather_y(level, starts):
         received(starts)
-        block = out_t.at[core, level, y]
-        return [links.start(block, block, y_peer[d]) for d in (2, 1, 3)]
-
-    def hand_over(level, starts):
-        received(starts)
+        for d in (2, 1, 3):
+            block = out_t.at[core, level, y]
+            links.start(
+                block, block, y_peer[d], out_sem.at[level, d], lambda: out_t.at[core, level, 0]
+            )
+
+    def hand_over(level):
+        for d in (2, 1, 3):
+            links.landed(out_t.at[core, level, y_of[d]], out_sem.at[level, d], mate)
         block = out_t.at[core, level]
         links.start(block, block, mate, hand_sem.at[level], lambda: out_t.at[core, level])
 
@@ -297,8 +300,9 @@
                 piece_sem.at[level, d, core], lambda: give.at[level, c],
             )
 
+    along_z(0, 1)
     along_y(0, 0)
-    along_z(0)
+    along_z(0, 2)
     for load in loads[2:6]:
         load.wait()
     theirs = grads.at[:, hi, x, :, bo_span]
@@ -309,7 +313,6 @@
     ]
     along_y(1, 0)
     bo_swap = links.start(bo.at[:, bo_span, :], bo.at[:, bo_span, :], mate)
-    bi_swap = [links.start(bi_hbm.at[level], bi.at[level, core], mate) for level in range(LAYERS)]
     for c in range(CORE):
         @pl.when(core == c)
         def _(c=c):
@@ -318,16 +321,20 @@
     segment = sort_segments()
 
     spread(0, 1)
-    along_z(1)
+    along_z(0, 3)
     pass_on(0, 0)
+    along_z(1, 1)
+    spread(0, 2)
+    along_z(1, 2)
     received(grads_in)
     block = grads.at[:, :, x]
     grads_x = [links.start(block, block, x_peer[d]) for d in (2, 1, 3)]
-    spread(0, 2)
     pass_on(0, 1)
+    bi_0 = links.start(bi_hbm.at[0], bi.at[0, core], mate)
     prepare(0)
     received([bo_swap])
     spread(0, 3)
+    along_z(1, 3)
     received(grads_x)
     out = [rotate_out(0), None]
     pass_on(0, 2)
@@ -335,33 +342,33 @@
     pass_on(1, 0)
     spread(1, 1)
     spread(1, 2)
+    bi_1 = links.start(bi_hbm.at[1], bi.at[1, core], mate)
     spread(1, 3)
-    out[1] = rotate_out(1)
     out[0] = add_y(0, out[0])
     gathered(0)
     loads[6].wait()
-    received(bi_swap[:1])
+    received([bi_0])
     rotate(0)
 
     pass_on(1, 1)
     pass_on(1, 2)
     out[0] = add_z(0, out[0])
     pass_on(1, 3)
-    out[1] = add_y(1, out[1])
-    out[0] = gather_y(0, out[0])
+    out[1] = rotate_out(1)
+    gather_y(0, out[0])
     add_x(0, 0)
     add_x(0, 1)
-    out[1] = add_z(1, out[1])
     prepare(1)
     gathered(1)
     loads[7].wait()
-    received(bi_swap[1:])
+    received([bi_1])
     rotate(1)
-    hand_over(0, out[0])
-    out[1] = gather_y(1, out[1])
+    out[1] = add_y(1, out[1])
+    hand_over(0)
     add_hi(0, 0)
     add_hi(0, 1)
     add_x(1, 0)
+    out[1] = add_z(1, out[1])
     handed(0)
 
 
@@ -375,14 +382,12 @@
         @pl.when(step == 1)
         def _():
             add_x(1, 1)
-            hand_over(1, out[1])
-
-        @pl.when(step == 3)
+            gather_y(1, out[1])
+
+        @pl.when(step == 4)
         def _():
             add_hi(1, 0)
-
-        @pl.when(step == 4)
-        def _():
+            hand_over(1)
             add_hi(1, 1)
             handed(1)
 
@@ -450,7 +455,9 @@
     received(ends)
     for d in range(Y - 1):
         total = total + er3[d]
-    out_ref[...] = total
+    own = half // (Z * Y)
+    total = pltpu.roll(total, lax.rem(half - (z * Y + y) * own, half), axis=1)
+    out_ref[...] = total.T[:own]
     links.finish()
 
 
@@ -500,10 +507,11 @@
         pltpu.SemaphoreType.DMA((LAYERS, CORE)),
         pltpu.SemaphoreType.DMA((LAYERS,)),
         pltpu.SemaphoreType.DMA((LAYERS,)),
+        pltpu.SemaphoreType.DMA((LAYERS, Y)),
     ]
     return pl.pallas_call(
         kernel,
-        out_shape=jax.ShapeDtypeStruct((QUERIES, half), F32),
+        out_shape=jax.ShapeDtypeStruct((half // (Z * Y), QUERIES), F32),
         in_specs=[pl.BlockSpec(memory_space=pl.ANY)] * 8,
         out_specs=pl.BlockSpec(memory_space=pltpu.VMEM),
         scratch_shapes=scratch,
@@ -517,7 +525,7 @@
 def on_device(
     train_acts, query_acts, train_grads, query_grads, basis_in, basis_out, eigen, query_segment
 ):
-    half = fused(
+    own = fused(
         train_acts.reshape(-1, ROWS_IN),
         query_acts.reshape(-1, ROWS_IN),
         train_grads,
@@ -527,9 +535,7 @@
         jnp.swapaxes(eigen, 1, 2),
         query_segment.reshape(1, TOK),
     )
-    own = TOK // (Z * Y * CORE)
-    start = lax.axis_index("seq") // CORE * own
-    return lax.dynamic_slice(half, (0, start), (QUERIES, own))
+    return jnp.swapaxes(own, 0, 1)
 
 
 def solution(mesh):

time: 82.4 us -> 80.9 us (0.982)
  Pallas kernels: 80.7 us -> 79.1 us
    pallas_call x1, Pallas kernels: 80.7 us -> 79.1 us  [fused(): pl.pallas_call(kernel, out_shape=jax.ShapeDtypeStruct((half // (Z * Y), Q...]
    dynamic_slice x2 -> x0, local copies, waits for them, and re-layouts: 1.44 us -> none  [on_device(): return lax.dynamic_slice(half, (0, start), (QUERIES, own))]
    unnamed x0 -> x1, local copies, waits for them, and re-layouts: none -> 1.28 us
where the time goes in v2:
time: 80.9 us; the launch traced here: 80.4 us
  Pallas kernels  79.1 us (98%)
  local copies, waits for them, and re-layouts  1.28 us (2%)
    pallas_call x1, Pallas kernels, fused(): pl.pallas_call(kernel, out_shape=jax.ShapeDtypeStruct((half // (Z * Y), Q...  79.1 us

profile of v2, /device:TPU:1, one launch (start us, length us, event | category | flops | bytes accessed | tf_op | source)
XLA Modules:
  0.0 80.4 jit_solution(17275232445000907291)
XLA Ops:
  0.0 79.1 %shard_map.82 = f32[8,16]{1,0:T(8,128)} custom-call(bf16[16,1792]{1,0:T(8,128)(2,1)} %bitcast.9, bf16[16,1792]{1,0:T(8,128)(2,1)} %bitcast.10, bf16[2,32,128]{2,1,0:T(8,128)(2,1)} %tg_hbm.1, bf16[2,32,128]{2,1,0:T(8,128)(2,1)} %qg_hbm.1, bf16[2,128,512]{2,1,0:T(8,128)(2,1)} %bo_hbm.1, s32[1,256]{1,0:T(1,128)} %bitcast.11, bf16[2,448,1792]{2,1,0:T(8,128)(2,1)} %bitcast.7, ...), custom_call_target="tpu_custom_call" | custom-call | flops 9400000512 | bytes 6000000 | tf_op jit(solution)/shard_map/pallas_call | solution.py:512
  79.1 1.3 %copy.10 = f32[16,8]{0,1:T(8,128)} copy(f32[16,8]{0,1:T(8,128)} %bitcast.6) | data formatting | bytes 1024

commit v3 on v2

--- a/solution.py
+++ b/solution.py
@@ -89,9 +89,9 @@
     out_ref,
     ta, qa, seg, bi, eig, tokens, acts, grads_s, grads, bo,
     part_out, own_out, ry, rz_s, rz, out_t,
-    part_in, rx_s, rx, zs, zr, give, rin,
+    part_in, rx_s, rx, zs, zm, zr, give, rin,
     scores, es1, er1, es2, er2, es3, er3,
-    local_sem, send_sem, recv_sem, z_sem, y_sem, on_sem, piece_sem, x_sem, hi_sem, hand_sem, give_sem, out_sem,
+    local_sem, send_sem, recv_sem, z_sem, y_sem, on_sem, piece_sem, x_sem, hi_sem, hand_sem, give_sem, out_sem, way_sem,
 ):
     li = lax.axis_index("layer")
     si = lax.axis_index("seq")
@@ -269,9 +269,24 @@
             total = total + rx[level, c, d].astype(F32)
         part_in[level, c, x] = total
         zs[level, c] = total.astype(BF16)
+        if level == 0:
+            links.start(
+                zs.at[level, c], zr.at[level, c], hi_peer, hi_sem.at[level, c],
+                lambda: zs.at[level, c],
+            )
+        else:
+            links.start(
+                zs.at[level, c], zm.at[c], ring_peer[way[c]], way_sem.at[c],
+                lambda: zs.at[level, c],
+            )
+
+    way = (2, 6)
+
+    def relay(level, c):
+        links.landed(zm.at[c], way_sem.at[c], mate)
         links.start(
-            zs.at[level, c], zr.at[level, c], hi_peer, hi_sem.at[level, c],
-            lambda: zs.at[level, c],
+            zm.at[c], zr.at[level, c], ring_peer[way[c]], hi_sem.at[level, c],
+            lambda: zm.at[c],
         )
 
     def add_hi(level, c):
@@ -383,6 +398,14 @@
         def _():
             add_x(1, 1)
             gather_y(1, out[1])
+
+        @pl.when(step == 2)
+        def _():
+            relay(1, 0)
+
+        @pl.when(step == 3)
+        def _():
+            relay(1, 1)
 
         @pl.when(step == 4)
         def _():
@@ -486,6 +509,7 @@
         pltpu.VMEM((LAYERS, 2, X, PIECE, TOK), BF16),
         pltpu.VMEM((LAYERS, 2, X - 1, PIECE, TOK), BF16),
         pltpu.VMEM((LAYERS, 2, PIECE, TOK), BF16),
+        pltpu.VMEM((CORE, PIECE, TOK), BF16),
         pltpu.VMEM((LAYERS, 2, PIECE, TOK), BF16),
         pltpu.VMEM((LAYERS, CORE, PIECE, TOK), BF16),
         pltpu.VMEM((LAYERS, 2, X, PIECE, TOK), BF16),
@@ -508,6 +532,7 @@
         pltpu.SemaphoreType.DMA((LAYERS,)),
         pltpu.SemaphoreType.DMA((LAYERS,)),
         pltpu.SemaphoreType.DMA((LAYERS, Y)),
+        pltpu.SemaphoreType.DMA((CORE,)),
     ]
     return pl.pallas_call(
         kernel,

time: 80.9 us -> 81.5 us (level)
  Pallas kernels: 79.1 us -> 80.1 us
    pallas_call x1, Pallas kernels: 79.1 us -> 80.1 us  [fused(): pl.pallas_call(kernel, out_shape=jax.ShapeDtypeStruct((half // (Z * Y), Q...]
where the time goes in v3:
time: 81.5 us; the launch traced here: 81.4 us
  Pallas kernels  80.1 us (98%)
  local copies, waits for them, and re-layouts  1.28 us (2%)
    pallas_call x1, Pallas kernels, fused(): pl.pallas_call(kernel, out_shape=jax.ShapeDtypeStruct((half // (Z * Y), Q...  80.1 us

profile of v3, /device:TPU:1, one launch (start us, length us, event | category | flops | bytes accessed | tf_op | source)
XLA Modules:
  0.0 81.4 jit_solution(11061580220010060925)
XLA Ops:
  0.0 80.1 %shard_map.82 = f32[8,16]{1,0:T(8,128)} custom-call(bf16[16,1792]{1,0:T(8,128)(2,1)} %bitcast.9, bf16[16,1792]{1,0:T(8,128)(2,1)} %bitcast.10, bf16[2,32,128]{2,1,0:T(8,128)(2,1)} %tg_hbm.1, bf16[2,32,128]{2,1,0:T(8,128)(2,1)} %qg_hbm.1, bf16[2,128,512]{2,1,0:T(8,128)(2,1)} %bo_hbm.1, s32[1,256]{1,0:T(1,128)} %bitcast.11, bf16[2,448,1792]{2,1,0:T(8,128)(2,1)} %bitcast.7, ...), custom_call_target="tpu_custom_call" | custom-call | flops 9400000512 | bytes 6000000 | tf_op jit(solution)/shard_map/pallas_call | solution.py:537
  80.1 1.3 %copy.10 = f32[16,8]{0,1:T(8,128)} copy(f32[16,8]{0,1:T(8,128)} %bitcast.6) | data formatting | bytes 1024

commit v4 on v2

--- a/solution.py
+++ b/solution.py
@@ -320,57 +320,57 @@
 
     segment = sort_segments()
 
+    along_z(0, 3)
     spread(0, 1)
-    along_z(0, 3)
+    spread(0, 2)
+    along_z(1, 1)
+    along_z(1, 2)
     pass_on(0, 0)
-    along_z(1, 1)
-    spread(0, 2)
-    along_z(1, 2)
     received(grads_in)
     block = grads.at[:, :, x]
     grads_x = [links.start(block, block, x_peer[d]) for d in (2, 1, 3)]
-    pass_on(0, 1)
+    spread(0, 3)
+    along_z(1, 3)
     bi_0 = links.start(bi_hbm.at[0], bi.at[0, core], mate)
     prepare(0)
+    pass_on(0, 1)
     received([bo_swap])
-    spread(0, 3)
-    along_z(1, 3)
     received(grads_x)
     out = [rotate_out(0), None]
-    pass_on(0, 2)
-    pass_on(0, 3)
-    pass_on(1, 0)
     spread(1, 1)
     spread(1, 2)
+    pass_on(0, 2)
+    pass_on(1, 0)
+    pass_on(0, 3)
+    spread(1, 3)
     bi_1 = links.start(bi_hbm.at[1], bi.at[1, core], mate)
-    spread(1, 3)
     out[0] = add_y(0, out[0])
+    pass_on(1, 1)
     gathered(0)
     loads[6].wait()
     received([bi_0])
     rotate(0)
 
-    pass_on(1, 1)
     pass_on(1, 2)
+    pass_on(1, 3)
     out[0] = add_z(0, out[0])
-    pass_on(1, 3)
     out[1] = rotate_out(1)
-    gather_y(0, out[0])
     add_x(0, 0)
-    add_x(0, 1)
     prepare(1)
     gathered(1)
     loads[7].wait()
     received([bi_1])
     rotate(1)
+    add_x(0, 1)
+    gather_y(0, out[0])
     out[1] = add_y(1, out[1])
+    add_x(1, 0)
     hand_over(0)
     add_hi(0, 0)
     add_hi(0, 1)
-    add_x(1, 0)
+    add_x(1, 1)
     out[1] = add_z(1, out[1])
     handed(0)
-
 
     scores[...] = jnp.zeros_like(scores)
 
@@ -381,7 +381,6 @@
 
         @pl.when(step == 1)
         def _():
-            add_x(1, 1)
             gather_y(1, out[1])
 
         @pl.when(step == 4)

time: 80.9 us -> 81.1 us (level)
  no operation moved by 1% of the time
where the time goes in v4:
time: 81.1 us; the launch traced here: 81 us
  Pallas kernels  79.7 us (98%)
  local copies, waits for them, and re-layouts  1.28 us (2%)
    pallas_call x1, Pallas kernels, fused(): pl.pallas_call(kernel, out_shape=jax.ShapeDtypeStruct((half // (Z * Y), Q...  79.7 us

profile of v4, /device:TPU:1, one launch (start us, length us, event | category | flops | bytes accessed | tf_op | source)
XLA Modules:
  0.0 81.0 jit_solution(4015229930670701665)
XLA Ops:
  0.0 79.7 %shard_map.82 = f32[8,16]{1,0:T(8,128)} custom-call(bf16[16,1792]{1,0:T(8,128)(2,1)} %bitcast.9, bf16[16,1792]{1,0:T(8,128)(2,1)} %bitcast.10, bf16[2,32,128]{2,1,0:T(8,128)(2,1)} %tg_hbm.1, bf16[2,32,128]{2,1,0:T(8,128)(2,1)} %qg_hbm.1, bf16[2,128,512]{2,1,0:T(8,128)(2,1)} %bo_hbm.1, s32[1,256]{1,0:T(1,128)} %bitcast.11, bf16[2,448,1792]{2,1,0:T(8,128)(2,1)} %bitcast.7, ...), custom_call_target="tpu_custom_call" | custom-call | flops 9400000512 | bytes 6000000 | tf_op jit(solution)/shard_map/pallas_call | solution.py:511
  79.7 1.3 %copy.10 = f32[16,8]{0,1:T(8,128)} copy(f32[16,8]{0,1:T(8,128)} %bitcast.6) | data formatting | bytes 1024

commit v5 on v4

--- a/solution.py
+++ b/solution.py
@@ -341,6 +341,7 @@
     spread(1, 2)
     pass_on(0, 2)
     pass_on(1, 0)
+    out[1] = rotate_out(1)
     pass_on(0, 3)
     spread(1, 3)
     bi_1 = links.start(bi_hbm.at[1], bi.at[1, core], mate)
@@ -352,24 +353,24 @@
     rotate(0)
 
     pass_on(1, 2)
+    out[1] = add_y(1, out[1])
     pass_on(1, 3)
     out[0] = add_z(0, out[0])
-    out[1] = rotate_out(1)
     add_x(0, 0)
     prepare(1)
+    gather_y(0, out[0])
+    out[1] = add_z(1, out[1])
     gathered(1)
     loads[7].wait()
     received([bi_1])
     rotate(1)
     add_x(0, 1)
-    gather_y(0, out[0])
-    out[1] = add_y(1, out[1])
-    add_x(1, 0)
+    gather_y(1, out[1])
     hand_over(0)
     add_hi(0, 0)
+    add_x(1, 0)
     add_hi(0, 1)
     add_x(1, 1)
-    out[1] = add_z(1, out[1])
     handed(0)
 
     scores[...] = jnp.zeros_like(scores)
@@ -379,14 +380,13 @@
         level, d = step // X, step % X
         at = lax.rem(x + X - d, X)
 
-        @pl.when(step == 1)
+        @pl.when(step == 2)
         def _():
-            gather_y(1, out[1])
+            hand_over(1)
 
         @pl.when(step == 4)
         def _():
             add_hi(1, 0)
-            hand_over(1)
             add_hi(1, 1)
             handed(1)
 

time: 81.1 us -> 82.2 us (1.014)
  Pallas kernels: 79.7 us -> 80.8 us
    pallas_call x1, Pallas kernels: 79.7 us -> 80.8 us  [fused(): pl.pallas_call(kernel, out_shape=jax.ShapeDtypeStruct((half // (Z * Y), Q...]
where the time goes in v5:
time: 82.2 us; the launch traced here: 82.1 us
  Pallas kernels  80.8 us (98%)
  local copies, waits for them, and re-layouts  1.28 us (2%)
    pallas_call x1, Pallas kernels, fused(): pl.pallas_call(kernel, out_shape=jax.ShapeDtypeStruct((half // (Z * Y), Q...  80.8 us

profile of v5, /device:TPU:1, one launch (start us, length us, event | category | flops | bytes accessed | tf_op | source)
XLA Modules:
  0.0 82.1 jit_solution(11100537534561562456)
XLA Ops:
  0.0 80.8 %shard_map.82 = f32[8,16]{1,0:T(8,128)} custom-call(bf16[16,1792]{1,0:T(8,128)(2,1)} %bitcast.9, bf16[16,1792]{1,0:T(8,128)(2,1)} %bitcast.10, bf16[2,32,128]{2,1,0:T(8,128)(2,1)} %tg_hbm.1, bf16[2,32,128]{2,1,0:T(8,128)(2,1)} %qg_hbm.1, bf16[2,128,512]{2,1,0:T(8,128)(2,1)} %bo_hbm.1, s32[1,256]{1,0:T(1,128)} %bitcast.11, bf16[2,448,1792]{2,1,0:T(8,128)(2,1)} %bitcast.7, ...), custom_call_target="tpu_custom_call" | custom-call | flops 9400000512 | bytes 6000000 | tf_op jit(solution)/shard_map/pallas_call | solution.py:511
  80.9 1.3 %copy.10 = f32[16,8]{0,1:T(8,128)} copy(f32[16,8]{0,1:T(8,128)} %bitcast.6) | data formatting | bytes 1024

commit v6 on v4

--- a/solution.py
+++ b/solution.py
@@ -25,7 +25,7 @@
 COLS_IN = FF // (Z * Y * CORE)
 ROWS_OUT = D // (Z * Y * CORE)
 COLS_OUT = D // (HI * X)
-COPIES = 128
+COPIES = 144
 PIECE = COLS_IN // X
 GROUP = 16
 VMEM_LIMIT = 62 * 1024 * 1024
@@ -90,7 +90,7 @@
     ta, qa, seg, bi, eig, tokens, acts, grads_s, grads, bo,
     part_out, own_out, ry, rz_s, rz, out_t,
     part_in, rx_s, rx, zs, zr, give, rin,
-    scores, es1, er1, es2, er2, es3, er3,
+    scores, es1, er1, es2, er2,
     local_sem, send_sem, recv_sem, z_sem, y_sem, on_sem, piece_sem, x_sem, hi_sem, hand_sem, give_sem, out_sem,
 ):
     li = lax.axis_index("layer")
@@ -115,10 +115,13 @@
     hi_peer = device(1 - hi, x, z, y, core)
     hi_other = device(1 - hi, x, z, y, other)
     ring_peer = [device(at // Z, x, at % Z, y, core) for at in ring_of]
+    ring_other = [device(at // Z, x, at % Z, y, other) for at in ring_of]
+    flat = [(dx, dy) for dx in (2, 1, 3, 0) for dy in (2, 1, 3, 0) if dx or dy]
+    flat_peer = [device(hi, x_of[dx], z, y_of[dy], core) for dx, dy in flat]
     links = Links(send_sem, recv_sem, mate)
 
     barrier = pltpu.get_barrier_semaphore()
-    peers = [mate, hi_other] + ring_peer[1:] + y_peer[1:] + x_peer[1:] + x_other[1:]
+    peers = ring_other + ring_peer[1:] + flat_peer + x_other[1:]
     for peer in peers:
         pl.semaphore_signal(barrier, inc=1, device_id=peer, device_id_type=MESH)
 
@@ -163,6 +166,8 @@
         block = acts.at[level, order[k], y]
         links.start(block, block, y_peer[1], y_sem.at[level, 0, order[k]])
         links.start(block, block, y_peer[3], y_sem.at[level, 1, order[k]])
+        if level == 1 and k >= 2:
+            links.start(block, block, y_peer[2], on_sem.at[level, order[k]])
 
     def spread(level, k):
         links.landed(acts.at[level, order[k], y], z_sem.at[level, order[k]], mate)
@@ -172,10 +177,11 @@
         left = acts.at[level, order[k], y_of[3]]
         right = acts.at[level, order[k], y_of[1]]
         links.landed(left, y_sem.at[level, 0, order[k]], mate)
-        if k % 2 == 0:
+        late = level == 1 and k >= 2
+        if k % 2 == 0 and not late:
             links.start(left, left, y_peer[1], on_sem.at[level, order[k]])
         links.landed(right, y_sem.at[level, 1, order[k]], mate)
-        if k % 2 == 1:
+        if k % 2 == 1 and not late:
             links.start(right, right, y_peer[3], on_sem.at[level, order[k]])
 
     def gathered(level):
@@ -351,12 +357,12 @@
     received([bi_0])
     rotate(0)
 
-    pass_on(1, 2)
-    pass_on(1, 3)
     out[0] = add_z(0, out[0])
     out[1] = rotate_out(1)
     add_x(0, 0)
     prepare(1)
+    pass_on(1, 2)
+    pass_on(1, 3)
     gathered(1)
     loads[7].wait()
     received([bi_1])
@@ -424,10 +430,10 @@
     es1[0] = summed[:, :half]
     es1[1] = summed[:, half:]
     ends = []
-    for d in (2, 1, 3):
-        ends.append(links.start(es1.at[other], er1.at[X - 1 + d], x_other[d]))
-        ends.append(links.start(es1.at[core], er1.at[d], x_peer[d]))
-    ends.append(links.start(es1.at[other], er1.at[0], mate))
+    for d in (4, 3, 5, 2, 6, 1, 7, 0):
+        ends.append(links.start(es1.at[other], er1.at[HI * Z + d], ring_other[d]))
+        if d:
+            ends.append(links.start(es1.at[core], er1.at[d], ring_peer[d]))
     links.finish()
     for level in range(LAYERS):
         pltpu.make_async_remote_copy(
@@ -439,21 +445,14 @@
             device_id_type=MESH,
         ).wait_send()
     received(ends)
-    total = es1[core]
-    for d in range(X * CORE - 1):
-        total = total + er1[d]
+    er1[0] = es1[core]
+    total = jnp.sum(er1[...], axis=0)
     es2[...] = total
     ends = []
-    for d in (4, 3, 5, 2, 6, 1, 7):
-        ends.append(links.start(es2, er2.at[d - 1], ring_peer[d]))
+    for at, (dx, dy) in enumerate(flat):
+        ends.append(links.start(es2, er2.at[at], flat_peer[at]))
     received(ends)
-    for d in range(HI * Z - 1):
-        total = total + er2[d]
-    es3[...] = total
-    ends = [links.start(es3, er3.at[d - 1], y_peer[d]) for d in (2, 1, 3)]
-    received(ends)
-    for d in range(Y - 1):
-        total = total + er3[d]
+    total = total + jnp.sum(er2[...], axis=0)
     own = half // (Z * Y)
     total = pltpu.roll(total, lax.rem(half - (z * Y + y) * own, half), axis=1)
     out_ref[...] = total.T[:own]
@@ -490,11 +489,9 @@
         pltpu.VMEM((LAYERS, 2, X, PIECE, TOK), BF16),
         pltpu.VMEM((QUERIES, 8, TOK), F32),
         pltpu.VMEM((2, QUERIES, half), F32),
-        pltpu.VMEM((HI * Z - 1, QUERIES, half), F32),
+        pltpu.VMEM((HI * Z * CORE, QUERIES, half), F32),
         pltpu.VMEM((QUERIES, half), F32),
-        pltpu.VMEM((Y * CORE - 1, QUERIES, half), F32),
-        pltpu.VMEM((QUERIES, half), F32),
-        pltpu.VMEM((X - 1, QUERIES, half), F32),
+        pltpu.VMEM((X * Y - 1, QUERIES, half), F32),
         pltpu.SemaphoreType.DMA((6 + 2 * LAYERS,)),
         pltpu.SemaphoreType.DMA((COPIES,)),
         pltpu.SemaphoreType.DMA((COPIES,)),

time: 81.1 us -> 81.9 us (level)
  no operation moved by 1% of the time
where the time goes in v6:
time: 81.9 us; the launch traced here: 81.8 us
  Pallas kernels  80.5 us (98%)
  local copies, waits for them, and re-layouts  1.28 us (2%)
    pallas_call x1, Pallas kernels, fused(): pl.pallas_call(kernel, out_shape=jax.ShapeDtypeStruct((half // (Z * Y), Q...  80.5 us

profile of v6, /device:TPU:1, one launch (start us, length us, event | category | flops | bytes accessed | tf_op | source)
XLA Modules:
  0.0 81.8 jit_solution(3477715032962956903)
XLA Ops:
  0.0 80.5 %shard_map.82 = f32[8,16]{1,0:T(8,128)} custom-call(bf16[16,1792]{1,0:T(8,128)(2,1)} %bitcast.9, bf16[16,1792]{1,0:T(8,128)(2,1)} %bitcast.10, bf16[2,32,128]{2,1,0:T(8,128)(2,1)} %tg_hbm.1, bf16[2,32,128]{2,1,0:T(8,128)(2,1)} %qg_hbm.1, bf16[2,128,512]{2,1,0:T(8,128)(2,1)} %bo_hbm.1, s32[1,256]{1,0:T(1,128)} %bitcast.11, bf16[2,448,1792]{2,1,0:T(8,128)(2,1)} %bitcast.7, ...), custom_call_target="tpu_custom_call" | custom-call | flops 9400000512 | bytes 6000000 | tf_op jit(solution)/shard_map/pallas_call | solution.py:508
  80.5 1.3 %copy.10 = f32[16,8]{0,1:T(8,128)} copy(f32[16,8]{0,1:T(8,128)} %bitcast.6) | data formatting | bytes 1024

commit v7 on v4

--- a/solution.py
+++ b/solution.py
@@ -25,7 +25,7 @@
 COLS_IN = FF // (Z * Y * CORE)
 ROWS_OUT = D // (Z * Y * CORE)
 COLS_OUT = D // (HI * X)
-COPIES = 128
+COPIES = 160
 PIECE = COLS_IN // X
 GROUP = 16
 VMEM_LIMIT = 62 * 1024 * 1024
@@ -145,7 +145,8 @@
         old = lax.broadcasted_iota(jnp.int32, (TOK, TOK), 0)
         new = lax.broadcasted_iota(jnp.int32, (TOK, TOK), 1)
         half = TOK // CORE
-        source = (new % half) // rows * (rows * CORE) + new // half * rows + new % rows
+        pair, far, odd = new % half // (half // 2), new % (half // 2) // 16, new % 16 // rows
+        source = (far * Y + pair * 2 + odd) * 16 + new // half * rows + new % rows
         pick = (old == source).astype(F32).astype(BF16)
         return jnp.dot(wide, pick, preferred_element_type=F32)[:1]
 
@@ -188,8 +189,8 @@
     def rotate_out(level):
         own = grads[level].reshape(TOK, CORE * ROWS_OUT)
         product = jnp.dot(own, bo[level], preferred_element_type=F32)
-        product = product.reshape(TOK // (CORE * rows), CORE, rows, COLS_OUT)
-        product = jnp.swapaxes(product, 0, 1).reshape(TOK, COLS_OUT)
+        product = product.reshape(Z, Y // 2, 2, CORE, rows, COLS_OUT)
+        product = jnp.transpose(product, (3, 1, 0, 2, 4, 5)).reshape(TOK, COLS_OUT)
         part_out[level] = product
         own_out[level] = product.astype(BF16).reshape(Y, y_rows, COLS_OUT)
         return [
@@ -238,66 +239,89 @@
         loads[8 + level].wait()
         eig[level] = factor / (eig[level] + DAMPING)
 
-    def rotate(level):
-        @pl.loop(0, TOK // 32)
-        def _(p):
-            pair = acts[level, p // (Y // 2), pl.ds(p % (Y // 2) * 2, 2)].astype(F32)
+    wide = TOK // 2
+    pairs = (y // 2, 1 - y // 2)
+
+    def lanes(slot):
+        if slot == 0:
+            return pl.ds(0, TOK)
+        return pl.ds(pl.multiple_of(pairs[slot - 1] * wide, wide), wide)
+
+    def sort(level, pair):
+        @pl.loop(0, Z)
+        def _(zz):
+            block = acts[level, zz, pl.ds(pair * 2, 2)].astype(F32)
             for at in range(2):
-                piece = pair[:, at * rows:(at + 1) * rows].reshape(2 * rows, ROWS_IN)
-                here = pl.ds(pl.multiple_of(at * (TOK // 2) + p * 2 * rows, 2 * rows), 2 * rows)
+                piece = block[:, at * rows:(at + 1) * rows].reshape(2 * rows, ROWS_IN)
+                here = pl.ds(pl.multiple_of(pair * wide + at * (wide // 2) + zz * 16, 16), 16)
                 tokens[here, :] = piece.astype(BF16)
+
+    def rotate(slot):
+        level = min(slot, 1)
+        if slot == 0:
+            sort(level, 0)
+            sort(level, 1)
+        else:
+            sort(level, pairs[slot - 1])
 
         @pl.loop(0, CORE)
         def _(c):
-            product = lax.dot_general(bi[level, c], tokens[...], NT, preferred_element_type=F32)
-            part_in[level, c] = product.reshape(X, PIECE, TOK)
-            rx_s[level, c] = product.astype(BF16).reshape(X, PIECE, TOK)
+            own = tokens[lanes(slot), :]
+            product = lax.dot_general(bi[level, c], own, NT, preferred_element_type=F32)
+            product = product.reshape(X, PIECE, product.shape[1])
+            part_in[level, c, :, :, lanes(slot)] = product
+            rx_s[level, c, :, :, lanes(slot)] = product.astype(BF16)
             for k in range(CORE):
                 @pl.when(c == k)
                 def _(k=k):
                     for d in (2, 1, 3):
                         links.start(
-                            rx_s.at[level, k, x_of[d]], rx.at[level, k, d - 1], x_peer[d],
-                            x_sem.at[level, k, d - 1], lambda: zs.at[level, k],
+                            rx_s.at[level, k, x_of[d], :, lanes(slot)],
+                            rx.at[level, k, d - 1, :, lanes(slot)],
+                            x_peer[d], x_sem.at[slot, k, d - 1],
+                            lambda: zs.at[level, k, :, lanes(slot)],
                         )
 
-    def add_x(level, c):
+    def add_x(slot, c):
+        level, here = min(slot, 1), lanes(slot)
         for d in range(X - 1):
-            links.landed(rx.at[level, c, d], x_sem.at[level, c, d], mate)
-        total = part_in[level, c, x]
+            links.landed(rx.at[level, c, d, :, here], x_sem.at[slot, c, d], mate)
+        total = part_in[level, c, x, :, here]
         for d in range(X - 1):
-            total = total + rx[level, c, d].astype(F32)
-        part_in[level, c, x] = total
-        zs[level, c] = total.astype(BF16)
+            total = total + rx[level, c, d, :, here].astype(F32)
+        part_in[level, c, x, :, here] = total
+        zs[level, c, :, here] = total.astype(BF16)
         links.start(
-            zs.at[level, c], zr.at[level, c], hi_peer, hi_sem.at[level, c],
-            lambda: zs.at[level, c],
+            zs.at[level, c, :, here], zr.at[level, c, :, here], hi_peer, hi_sem.at[slot, c],
+            lambda: zs.at[level, c, :, lanes(slot)],
         )
 
-    def add_hi(level, c):
-        links.landed(zr.at[level, c], hi_sem.at[level, c], mate)
-        total = part_in[level, c, x] + zr[level, c].astype(F32)
-        give[level, c] = total.astype(BF16)
+    def add_hi(slot, c):
+        level, here = min(slot, 1), lanes(slot)
+        links.landed(zr.at[level, c, :, here], hi_sem.at[slot, c], mate)
+        total = part_in[level, c, x, :, here] + zr[level, c, :, here].astype(F32)
+        give[level, c, :, here] = total.astype(BF16)
 
         @pl.when(core == c)
         def _():
-            rin[level, core, x] = give[level, c]
+            rin[level, core, x, :, lanes(slot)] = give[level, c, :, lanes(slot)]
 
         @pl.when(core != c)
         def _():
             pltpu.make_async_remote_copy(
-                src_ref=give.at[level, c],
-                dst_ref=rin.at[level, core, x],
-                send_sem=give_sem.at[level],
-                recv_sem=piece_sem.at[level, 0, core],
+                src_ref=give.at[level, c, :, lanes(slot)],
+                dst_ref=rin.at[level, core, x, :, lanes(slot)],
+                send_sem=give_sem.at[slot],
+                recv_sem=piece_sem.at[slot, 0, core],
                 device_id=mate,
                 device_id_type=MESH,
             ).start()
 
         for d in (1, 2, 3):
             links.start(
-                give.at[level, c], rin.at[level, core, x], device(hi, x_of[d], z, y, c),
-                piece_sem.at[level, d, core], lambda: give.at[level, c],
+                give.at[level, c, :, here], rin.at[level, core, x, :, here],
+                device(hi, x_of[d], z, y, c), piece_sem.at[slot, d, core],
+                lambda: give.at[level, c, :, lanes(slot)],
             )
 
     along_z(0, 1)
@@ -353,22 +377,25 @@
 
     pass_on(1, 2)
     pass_on(1, 3)
+    loads[7].wait()
+    received([bi_1])
+    rotate(1)
     out[0] = add_z(0, out[0])
     out[1] = rotate_out(1)
     add_x(0, 0)
     prepare(1)
     gathered(1)
-    loads[7].wait()
-    received([bi_1])
-    rotate(1)
+    rotate(2)
     add_x(0, 1)
+    add_x(1, 0)
+    add_x(1, 1)
     gather_y(0, out[0])
     out[1] = add_y(1, out[1])
-    add_x(1, 0)
+    add_x(2, 0)
     hand_over(0)
     add_hi(0, 0)
     add_hi(0, 1)
-    add_x(1, 1)
+    add_x(2, 1)
     out[1] = add_z(1, out[1])
     handed(0)
 
@@ -383,22 +410,45 @@
         def _():
             gather_y(1, out[1])
 
+        @pl.when(step == 3)
+        def _():
+            add_hi(1, 0)
+            add_hi(1, 1)
+
         @pl.when(step == 4)
         def _():
-            add_hi(1, 0)
+            add_hi(2, 0)
             hand_over(1)
-            add_hi(1, 1)
+            add_hi(2, 1)
             handed(1)
 
-        links.landed(rin.at[level, other, at], piece_sem.at[level, d, other], mate)
+        def arrived(stream):
+            @pl.when(level == 0)
+            def _():
+                links.landed(rin.at[0, stream, at], piece_sem.at[0, d, stream], mate)
+
+            @pl.when(level == 1)
+            def _():
+                for slot in (1, 2):
+                    links.landed(
+                        rin.at[1, stream, at, :, lanes(slot)], piece_sem.at[slot, d, stream], mate
+                    )
+
+        arrived(other)
 
         @pl.when(d != 0)
         def _():
-            links.landed(rin.at[level, core, at], piece_sem.at[level, d, core], mate)
-
-        both = [rin[level, c, at] for c in range(CORE)]
-        train_in = jnp.concatenate([b[:, :TOK // 2] for b in both], axis=1).astype(F32)
-        query_in = jnp.concatenate([b[:, TOK // 2:] for b in both], axis=1)
+            arrived(core)
+
+        low = lax.broadcasted_iota(jnp.int32, (PIECE, wide), 1) < wide // 2
+        train_in, query_in = [], []
+        for c in range(CORE):
+            both = rin[level, c, at].astype(F32)
+            one, two = both[:, :wide], both[:, wide:]
+            train_in.append(jnp.where(low, one, pltpu.roll(two, wide // 2, axis=1)))
+            query_in.append(jnp.where(low, pltpu.roll(one, wide // 2, axis=1), two))
+        train_in = jnp.concatenate(train_in, axis=1)
+        query_in = jnp.concatenate(query_in, axis=1).astype(BF16)
         scale = eig[level, pl.ds(pl.multiple_of(at * PIECE, PIECE), PIECE), :]
         query_out = out_t[1, level].reshape(TOK, COLS_OUT)
         train_out = out_t[0, level].reshape(TOK, COLS_OUT)
@@ -429,11 +479,12 @@
         ends.append(links.start(es1.at[core], er1.at[d], x_peer[d]))
     ends.append(links.start(es1.at[other], er1.at[0], mate))
     links.finish()
-    for level in range(LAYERS):
+    for slot in range(LAYERS + 1):
+        block = give.at[min(slot, 1), 0, :, lanes(slot)]
         pltpu.make_async_remote_copy(
-            src_ref=give.at[level, 0],
-            dst_ref=give.at[level, 0],
-            send_sem=give_sem.at[level],
+            src_ref=block,
+            dst_ref=block,
+            send_sem=give_sem.at[slot],
             recv_sem=recv_sem.at[0],
             device_id=mate,
             device_id_type=MESH,
@@ -455,7 +506,7 @@
     for d in range(Y - 1):
         total = total + er3[d]
     own = half // (Z * Y)
-    total = pltpu.roll(total, lax.rem(half - (z * Y + y) * own, half), axis=1)
+    total = pltpu.roll(total, lax.rem(half - (y // 2 * Z * 2 + z * 2 + y % 2) * own, half), axis=1)
     out_ref[...] = total.T[:own]
     links.finish()
 
@@ -501,11 +552,11 @@
         pltpu.SemaphoreType.DMA((LAYERS, Z)),
         pltpu.SemaphoreType.DMA((LAYERS, 2, Z)),
         pltpu.SemaphoreType.DMA((LAYERS, Z)),
-        pltpu.SemaphoreType.DMA((LAYERS, X, 2)),
-        pltpu.SemaphoreType.DMA((LAYERS, CORE, X - 1)),
-        pltpu.SemaphoreType.DMA((LAYERS, CORE)),
+        pltpu.SemaphoreType.DMA((LAYERS + 1, X, 2)),
+        pltpu.SemaphoreType.DMA((LAYERS + 1, CORE, X - 1)),
+        pltpu.SemaphoreType.DMA((LAYERS + 1, CORE)),
         pltpu.SemaphoreType.DMA((LAYERS,)),
-        pltpu.SemaphoreType.DMA((LAYERS,)),
+        pltpu.SemaphoreType.DMA((LAYERS + 1,)),
         pltpu.SemaphoreType.DMA((LAYERS, Y)),
     ]
     return pl.pallas_call(

time: 81.1 us -> 82.5 us (1.017)
  Pallas kernels: 79.7 us -> 80.6 us
    pallas_call x1, Pallas kernels: 79.7 us -> 80.6 us  [fused(): pl.pallas_call(kernel, out_shape=jax.ShapeDtypeStruct((half // (Z * Y), Q...]
where the time goes in v7:
time: 82.5 us; the launch traced here: 81.9 us
  Pallas kernels  80.6 us (98%)
  local copies, waits for them, and re-layouts  1.28 us (2%)
    pallas_call x1, Pallas kernels, fused(): pl.pallas_call(kernel, out_shape=jax.ShapeDtypeStruct((half // (Z * Y), Q...  80.6 us

profile of v7, /device:TPU:1, one launch (start us, length us, event | category | flops | bytes accessed | tf_op | source)
XLA Modules:
  0.0 81.9 jit_solution(11183452772743005503)
XLA Ops:
  0.0 80.6 %shard_map.82 = f32[8,16]{1,0:T(8,128)} custom-call(bf16[16,1792]{1,0:T(8,128)(2,1)} %bitcast.9, bf16[16,1792]{1,0:T(8,128)(2,1)} %bitcast.10, bf16[2,32,128]{2,1,0:T(8,128)(2,1)} %tg_hbm.1, bf16[2,32,128]{2,1,0:T(8,128)(2,1)} %qg_hbm.1, bf16[2,128,512]{2,1,0:T(8,128)(2,1)} %bo_hbm.1, s32[1,256]{1,0:T(1,128)} %bitcast.11, bf16[2,448,1792]{2,1,0:T(8,128)(2,1)} %bitcast.7, ...), custom_call_target="tpu_custom_call" | custom-call | flops 9400000512 | bytes 6000000 | tf_op jit(solution)/shard_map/pallas_call | solution.py:562
  80.6 1.3 %copy.10 = f32[16,8]{0,1:T(8,128)} copy(f32[16,8]{0,1:T(8,128)} %bitcast.6) | data formatting | bytes 1024

commit v8 on v4

--- a/solution.py
+++ b/solution.py
@@ -91,7 +91,7 @@
     part_out, own_out, ry, rz_s, rz, out_t,
     part_in, rx_s, rx, zs, zr, give, rin,
     scores, es1, er1, es2, er2, es3, er3,
-    local_sem, send_sem, recv_sem, z_sem, y_sem, on_sem, piece_sem, x_sem, hi_sem, hand_sem, give_sem, out_sem,
+    local_sem, send_sem, recv_sem, z_sem, y_sem, on_sem, piece_sem, x_sem, hi_sem, hand_sem, give_sem, out_sem, pass_sem,
 ):
     li = lax.axis_index("layer")
     si = lax.axis_index("seq")
@@ -155,9 +155,41 @@
     farthest = 3 * (1 - z // 2)
     order = [z, nearest, 6 - z - nearest - farthest, farthest]
 
-    def along_z(level, k):
-        block = acts.at[level, z, y]
-        links.start(block, block, device(hi, x, order[k], y, core), z_sem.at[level, z])
+    inner = z * (Z - 1 - z) > 0
+
+    def to_z(level, at, zz, slot):
+        block = acts.at[level, at, y]
+        return pltpu.make_async_remote_copy(
+            src_ref=block,
+            dst_ref=block,
+            send_sem=pass_sem.at[level, slot],
+            recv_sem=z_sem.at[level, at],
+            device_id=device(hi, x, zz, y, core),
+            device_id_type=MESH,
+        )
+
+    def along_z(level):
+        @pl.when(z > 0)
+        def _():
+            to_z(level, z, z - 1, 0).start()
+
+        @pl.when(z < Z - 1)
+        def _():
+            to_z(level, z, z + 1, 1).start()
+
+    def sent_z(level):
+        @pl.when(z > 0)
+        def _():
+            to_z(level, z, z - 1, 0).wait_send()
+
+        @pl.when(z < Z - 1)
+        def _():
+            to_z(level, z, z + 1, 1).wait_send()
+
+        @pl.when(inner)
+        def _():
+            for k in range(1, Z):
+                to_z(level, order[k], z - 1, 1 + k).wait_send()
 
     def along_y(level, k):
         block = acts.at[level, order[k], y]
@@ -166,6 +198,12 @@
 
     def spread(level, k):
         links.landed(acts.at[level, order[k], y], z_sem.at[level, order[k]], mate)
+
+        @pl.when(inner)
+        def _():
+            onward = z + 1 - 2 * ((order[k] + Z - z) // Z)
+            to_z(level, order[k], onward, 1 + k).start()
+
         along_y(level, k)
 
     def pass_on(level, k):
@@ -300,9 +338,8 @@
                 piece_sem.at[level, d, core], lambda: give.at[level, c],
             )
 
-    along_z(0, 1)
+    along_z(0)
     along_y(0, 0)
-    along_z(0, 2)
     for load in loads[2:6]:
         load.wait()
     theirs = grads.at[:, hi, x, :, bo_span]
@@ -320,20 +357,17 @@
 
     segment = sort_segments()
 
-    along_z(0, 3)
     spread(0, 1)
     spread(0, 2)
-    along_z(1, 1)
-    along_z(1, 2)
+    along_z(1)
     pass_on(0, 0)
     received(grads_in)
     block = grads.at[:, :, x]
     grads_x = [links.start(block, block, x_peer[d]) for d in (2, 1, 3)]
+    pass_on(0, 1)
     spread(0, 3)
-    along_z(1, 3)
     bi_0 = links.start(bi_hbm.at[0], bi.at[0, core], mate)
     prepare(0)
-    pass_on(0, 1)
     received([bo_swap])
     received(grads_x)
     out = [rotate_out(0), None]
@@ -351,25 +385,24 @@
     received([bi_0])
     rotate(0)
 
-    pass_on(1, 2)
-    pass_on(1, 3)
     out[0] = add_z(0, out[0])
     out[1] = rotate_out(1)
+    pass_on(1, 2)
     add_x(0, 0)
+    pass_on(1, 3)
+    gather_y(0, out[0])
+    add_x(0, 1)
     prepare(1)
+    out[1] = add_y(1, out[1])
     gathered(1)
     loads[7].wait()
     received([bi_1])
     rotate(1)
-    add_x(0, 1)
-    gather_y(0, out[0])
-    out[1] = add_y(1, out[1])
-    add_x(1, 0)
     hand_over(0)
     add_hi(0, 0)
+    out[1] = add_z(1, out[1])
     add_hi(0, 1)
-    add_x(1, 1)
-    out[1] = add_z(1, out[1])
+    add_x(1, 0)
     handed(0)
 
     scores[...] = jnp.zeros_like(scores)
@@ -381,12 +414,16 @@
 
         @pl.when(step == 1)
         def _():
+            add_x(1, 1)
             gather_y(1, out[1])
 
+        @pl.when(step == 3)
+        def _():
+            hand_over(1)
+
         @pl.when(step == 4)
         def _():
             add_hi(1, 0)
-            hand_over(1)
             add_hi(1, 1)
             handed(1)
 
@@ -430,6 +467,7 @@
     ends.append(links.start(es1.at[other], er1.at[0], mate))
     links.finish()
     for level in range(LAYERS):
+        sent_z(level)
         pltpu.make_async_remote_copy(
             src_ref=give.at[level, 0],
             dst_ref=give.at[level, 0],
@@ -507,6 +545,7 @@
         pltpu.SemaphoreType.DMA((LAYERS,)),
         pltpu.SemaphoreType.DMA((LAYERS,)),
         pltpu.SemaphoreType.DMA((LAYERS, Y)),
+        pltpu.SemaphoreType.DMA((LAYERS, 1 + Z)),
     ]
     return pl.pallas_call(
         kernel,

time: 81.1 us -> 80.2 us (0.989)
  Pallas kernels: 79.7 us -> 78.8 us
    pallas_call x1, Pallas kernels: 79.7 us -> 78.8 us  [fused(): pl.pallas_call(kernel, out_shape=jax.ShapeDtypeStruct((half // (Z * Y), Q...]
where the time goes in v8:
time: 80.2 us; the launch traced here: 80.1 us
  Pallas kernels  78.8 us (98%)
  local copies, waits for them, and re-layouts  1.28 us (2%)
    pallas_call x1, Pallas kernels, fused(): pl.pallas_call(kernel, out_shape=jax.ShapeDtypeStruct((half // (Z * Y), Q...  78.8 us

profile of v8, /device:TPU:1, one launch (start us, length us, event | category | flops | bytes accessed | tf_op | source)
XLA Modules:
  0.0 80.1 jit_solution(5978482328476344425)
XLA Ops:
  0.0 78.8 %shard_map.82 = f32[8,16]{1,0:T(8,128)} custom-call(bf16[16,1792]{1,0:T(8,128)(2,1)} %bitcast.9, bf16[16,1792]{1,0:T(8,128)(2,1)} %bitcast.10, bf16[2,32,128]{2,1,0:T(8,128)(2,1)} %tg_hbm.1, bf16[2,32,128]{2,1,0:T(8,128)(2,1)} %qg_hbm.1, bf16[2,128,512]{2,1,0:T(8,128)(2,1)} %bo_hbm.1, s32[1,256]{1,0:T(1,128)} %bitcast.11, bf16[2,448,1792]{2,1,0:T(8,128)(2,1)} %bitcast.7, ...), custom_call_target="tpu_custom_call" | custom-call | flops 9400000512 | bytes 6000000 | tf_op jit(solution)/shard_map/pallas_call | solution.py:550
  78.8 1.3 %copy.10 = f32[16,8]{0,1:T(8,128)} copy(f32[16,8]{0,1:T(8,128)} %bitcast.6) | data formatting | bytes 1024

commit v9 on v8

--- a/solution.py
+++ b/solution.py
@@ -405,6 +405,16 @@
     add_x(1, 0)
     handed(0)
 
+    def given(level):
+        pltpu.make_async_remote_copy(
+            src_ref=give.at[level, 0],
+            dst_ref=give.at[level, 0],
+            send_sem=give_sem.at[level],
+            recv_sem=recv_sem.at[0],
+            device_id=mate,
+            device_id_type=MESH,
+        ).wait_send()
+
     scores[...] = jnp.zeros_like(scores)
 
     @pl.loop(0, LAYERS * X)
@@ -423,6 +433,10 @@
 
         @pl.when(step == 4)
         def _():
+            links.finish()
+            for side in range(LAYERS):
+                sent_z(side)
+            given(0)
             add_hi(1, 0)
             add_hi(1, 1)
             handed(1)
@@ -466,16 +480,7 @@
         ends.append(links.start(es1.at[core], er1.at[d], x_peer[d]))
     ends.append(links.start(es1.at[other], er1.at[0], mate))
     links.finish()
-    for level in range(LAYERS):
-        sent_z(level)
-        pltpu.make_async_remote_copy(
-            src_ref=give.at[level, 0],
-            dst_ref=give.at[level, 0],
-            send_sem=give_sem.at[level],
-            recv_sem=recv_sem.at[0],
-            device_id=mate,
-            device_id_type=MESH,
-        ).wait_send()
+    given(1)
     received(ends)
     total = es1[core]
     for d in range(X * CORE - 1):

time: 80.2 us -> 80.3 us (level)
  no operation moved by 1% of the time
where the time goes in v9:
time: 80.3 us; the launch traced here: 80.2 us
  Pallas kernels  78.9 us (98%)
  local copies, waits for them, and re-layouts  1.28 us (2%)
    pallas_call x1, Pallas kernels, fused(): pl.pallas_call(kernel, out_shape=jax.ShapeDtypeStruct((half // (Z * Y), Q...  78.9 us

profile of v9, /device:TPU:1, one launch (start us, length us, event | category | flops | bytes accessed | tf_op | source)
XLA Modules:
  0.0 80.2 jit_solution(2001627511928465360)
XLA Ops:
  0.0 78.9 %shard_map.82 = f32[8,16]{1,0:T(8,128)} custom-call(bf16[16,1792]{1,0:T(8,128)(2,1)} %bitcast.9, bf16[16,1792]{1,0:T(8,128)(2,1)} %bitcast.10, bf16[2,32,128]{2,1,0:T(8,128)(2,1)} %tg_hbm.1, bf16[2,32,128]{2,1,0:T(8,128)(2,1)} %qg_hbm.1, bf16[2,128,512]{2,1,0:T(8,128)(2,1)} %bo_hbm.1, s32[1,256]{1,0:T(1,128)} %bitcast.11, bf16[2,448,1792]{2,1,0:T(8,128)(2,1)} %bitcast.7, ...), custom_call_target="tpu_custom_call" | custom-call | flops 9400000512 | bytes 6000000 | tf_op jit(solution)/shard_map/pallas_call | solution.py:555
  79.0 1.3 %copy.10 = f32[16,8]{0,1:T(8,128)} copy(f32[16,8]{0,1:T(8,128)} %bitcast.6) | data formatting | bytes 1024

commit v10 on v9

--- a/solution.py
+++ b/solution.py
@@ -403,6 +403,7 @@
     out[1] = add_z(1, out[1])
     add_hi(0, 1)
     add_x(1, 0)
+    add_x(1, 1)
     handed(0)
 
     def given(level):
@@ -424,7 +425,6 @@
 
         @pl.when(step == 1)
         def _():
-            add_x(1, 1)
             gather_y(1, out[1])
 
         @pl.when(step == 3)

time: 80.3 us -> 80.7 us (level)
  no operation moved by 1% of the time
where the time goes in v10:
time: 80.7 us; the launch traced here: 80.6 us
  Pallas kernels  79.3 us (98%)
  local copies, waits for them, and re-layouts  1.28 us (2%)
    pallas_call x1, Pallas kernels, fused(): pl.pallas_call(kernel, out_shape=jax.ShapeDtypeStruct((half // (Z * Y), Q...  79.3 us

profile of v10, /device:TPU:1, one launch (start us, length us, event | category | flops | bytes accessed | tf_op | source)
XLA Modules:
  0.0 80.6 jit_solution(18195663612980450935)
XLA Ops:
  0.0 79.3 %shard_map.82 = f32[8,16]{1,0:T(8,128)} custom-call(bf16[16,1792]{1,0:T(8,128)(2,1)} %bitcast.9, bf16[16,1792]{1,0:T(8,128)(2,1)} %bitcast.10, bf16[2,32,128]{2,1,0:T(8,128)(2,1)} %tg_hbm.1, bf16[2,32,128]{2,1,0:T(8,128)(2,1)} %qg_hbm.1, bf16[2,128,512]{2,1,0:T(8,128)(2,1)} %bo_hbm.1, s32[1,256]{1,0:T(1,128)} %bitcast.11, bf16[2,448,1792]{2,1,0:T(8,128)(2,1)} %bitcast.7, ...), custom_call_target="tpu_custom_call" | custom-call | flops 9400000512 | bytes 6000000 | tf_op jit(solution)/shard_map/pallas_call | solution.py:555
  79.3 1.3 %copy.10 = f32[16,8]{0,1:T(8,128)} copy(f32[16,8]{0,1:T(8,128)} %bitcast.6) | data formatting | bytes 1024
